TPU v7x, 128 devices: a whole 4x4x4 slice. The times are simulated.
128 devices in a mesh: dom: 16 (over x, z_hi, core), space: 8 (over y, z_lo).
Axes of the slice: x: 4, y: 4, z: 4 (z_hi: 2, z_lo: 2; z = z_hi * 2 + z_lo), core: 2. Of those that a mesh axis runs over, the one named last changes fastest.
Arguments:
- particles: float32 [32, 3, 512, 1024], P('dom', None, 'space'), may hold values from -6 to 6
- copies: int32 [32], replicated, may hold values from 0 to 31
- depth_class: int32 [512, 1024], P('space'), may hold values from 0 to 7
- depth_table: float32 [8], replicated, may hold values from 0.5 to 2
- observed: float32 [512, 1024], P('space'), may hold values from -6 to 6
- nudge_gain: float32 [512, 1024], P('space'), may hold values from 0.02 to 0.3
Outputs:
- advanced: float32 [32, 3, 512, 1024], P('dom', None, 'space')
All inputs are finite; a program needn't handle non-finite values.
Results may differ from a plain program's by a relative error of at most 0.00002.
Values sent between devices are 32-bit elements; how exact they have to be, the bound alone decides.
A program may use at most 128 MiB of HBM per device.

v0:
```python
import functools

import jax
import jax.numpy as jnp
from jax import lax
from jax.experimental import pallas as pl
from jax.experimental.pallas import tpu as pltpu
from jax.sharding import PartitionSpec as P

MESH = pl.DeviceIdType.MESH
STEPS = 4
CLASSES = 8
ROWS = 64
PANELS = 8
PAD = 16
TILES = ROWS // 8
DT = 0.3
F0 = 0.3
K = DT / 12.0

GROUP = 16


def peer_of(me, i):
    step = (i * 7) % GROUP
    x, z, c = me // 4 + step // 4, me // 2 + step // 2, me + step
    return (x % 4) * 4 + (z % 2) * 2 + c % 2


def row_of(piece, d):
    tile = 2 + d // 4 if piece == 0 else d // 4 + 4 * (d // 8)
    return pl.multiple_of(tile * 8, 8)


def quarter_of(d):
    return d % 4


def kernel(
    copies_in, table_in, particles, classes, observed, gain, out,
    copies, table, stage, cls, obs, gn, depth, keep, drive, state, flux, part, part_flux, gathered0, gathered1, chosen, sent, got,
    load_sem, halo_ss, halo_rs, fixed_ss, fixed_rs, ss1, rs1, ss2, rs2, self_sem,
):
    me, sp = lax.axis_index("dom"), lax.axis_index("space")
    gathered = (gathered0, gathered1)
    up, down = (sp + 7) % 8, (sp + 1) % 8

    loads = [
        pltpu.make_async_copy(classes, cls, load_sem.at[0]),
        pltpu.make_async_copy(particles, stage, load_sem.at[1]),
        pltpu.make_async_copy(gain, gn, load_sem.at[2]),
        pltpu.make_async_copy(observed, obs, load_sem.at[3]),
        pltpu.make_async_copy(table_in, table, load_sem.at[4]),
        pltpu.make_async_copy(copies_in, copies, load_sem.at[5]),
    ]
    for load in loads:
        load.start()

    barrier = pltpu.get_barrier_semaphore()

    @pl.loop(1, GROUP)
    def _(i):
        pl.semaphore_signal(barrier, inc=1, device_id=(peer_of(me, i), sp), device_id_type=MESH)

    for other in (up, down):
        pl.semaphore_signal(barrier, inc=1, device_id=(me, other), device_id_type=MESH)

    lane = lax.broadcasted_iota(jnp.int32, (8, 128), 1)
    sublane = lax.broadcasted_iota(jnp.int32, (8, 128), 0)

    loads[0].wait()
    loads[4].wait()

    @pl.loop(0, TILES)
    def _(t):
        base = pl.multiple_of(t * 8, 8)
        for c in range(PANELS):
            kind = cls[pl.ds(base, 8), c * 128 : c * 128 + 128]
            d = jnp.zeros((8, 128), jnp.float32)
            for klass in range(CLASSES):
                d = jnp.where(kind == klass, table[klass], d)
            depth[c, pl.ds(base + PAD, 8), :] = d

    loads[1].wait()

    @pl.loop(0, 2 * TILES)
    def _(i):
        p, t = i // TILES, i % TILES
        base = pl.multiple_of(t * 8, 8)
        for c in range(PANELS):
            for f in range(3):
                v = stage[p, f, pl.ds(base, 8), c * 128 : c * 128 + 128]
                state[p, f, c, pl.ds(base + PAD, 8), :] = v
                if f == 2:
                    flux[p, c, pl.ds(base + PAD, 8), :] = depth[c, pl.ds(base + PAD, 8), :] * v

    none = jnp.zeros((8, 128), jnp.float32)

    @pl.loop(0, 4)
    def _(i):
        row = pl.multiple_of((i % 2) * 8 + (i // 2) * (ROWS + PAD), 8)
        for c in range(PANELS):
            drive[c, pl.ds(row, 8), :] = none
            for p in range(2):
                flux[p, c, pl.ds(row, 8), :] = none
                for f in range(3):
                    state[p, f, c, pl.ds(row, 8), :] = none
        for side in range(2):
            for p in range(2):
                for c in range(PANELS):
                    part_flux[side, p, c, pl.ds(pl.multiple_of(i * 8, 8), 8), :] = none
                    for f in range(3):
                        part[side, p, f, c, pl.ds(pl.multiple_of(i * 8, 8), 8), :] = none

    loads[2].wait()
    loads[3].wait()
    loads[5].wait()

    @pl.loop(0, TILES)
    def _(t):
        base = pl.multiple_of(t * 8, 8)
        for c in range(PANELS):
            g = gn[pl.ds(base, 8), c * 128 : c * 128 + 128]
            keep[c, pl.ds(base + PAD, 8), :] = 1.0 - g
            drive[c, pl.ds(base + PAD, 8), :] = g * obs[pl.ds(base, 8), c * 128 : c * 128 + 128]

    def shifts(panels):
        ahead = [pltpu.roll(v, 127, 1) for v in panels]
        ahead2 = [pltpu.roll(v, 126, 1) for v in panels]
        behind = [pltpu.roll(v, 1, 1) for v in panels]
        behind2 = [pltpu.roll(v, 2, 1) for v in panels]
        found = []
        for c in range(PANELS):
            nxt, prv = (c + 1) % PANELS, (c - 1) % PANELS
            found.append((
                jnp.where(lane < 127, ahead[c], ahead[nxt]),
                jnp.where(lane >= 1, behind[c], behind[prv]),
                jnp.where(lane < 126, ahead2[c], ahead2[nxt]),
                jnp.where(lane >= 2, behind2[c], behind2[prv]),
            ))
        return found

    def columns_of(panels):
        return [8.0 * (a - b) - (a2 - b2) for a, b, a2, b2 in shifts(panels)]

    def heights_of(base, low, high):
        inside = (base + sublane >= low) & (base + sublane < high)
        here = pl.ds(base + PAD, 8)
        found = []
        for p in range(2):
            columns = columns_of([depth[c, here, :] * state[p, 1, c, here, :] for c in range(PANELS)])
            for c, along in enumerate(columns):
                a = flux[p, c, pl.ds(base + PAD + 1, 8), :]
                b = flux[p, c, pl.ds(base + PAD - 1, 8), :]
                a2 = flux[p, c, pl.ds(base + PAD + 2, 8), :]
                b2 = flux[p, c, pl.ds(base + PAD - 2, 8), :]
                old = state[p, 0, c, here, :]
                h = old - K * (along + (8.0 * (a - b) - (a2 - b2)))
                h = keep[c, here, :] * h + drive[c, here, :]
                found.append((p, c, jnp.where(inside, h, old)))
        return found

    def put_heights(base, low, high):
        for p, c, h in heights_of(base, low, high):
            state[p, 0, c, pl.ds(base + PAD, 8), :] = h

    def velocities_of(base):
        here = pl.ds(base + PAD, 8)
        found = []
        for p in range(2):
            for c, along in enumerate(columns_of([state[p, 0, c, here, :] for c in range(PANELS)])):
                a = state[p, 0, c, pl.ds(base + PAD + 1, 8), :]
                b = state[p, 0, c, pl.ds(base + PAD - 1, 8), :]
                a2 = state[p, 0, c, pl.ds(base + PAD + 2, 8), :]
                b2 = state[p, 0, c, pl.ds(base + PAD - 2, 8), :]
                e, n = state[p, 1, c, here, :], state[p, 2, c, here, :]
                e_new = e - K * along + (DT * F0) * n
                n_new = n - K * (8.0 * (a - b) - (a2 - b2)) - (DT * F0) * e
                found.append((p, c, e_new, n_new, depth[c, here, :] * n_new))
        return found

    def put_velocities(base):
        for p, c, e, n, f in velocities_of(base):
            state[p, 1, c, pl.ds(base + PAD, 8), :] = e
            state[p, 2, c, pl.ds(base + PAD, 8), :] = n
            flux[p, c, pl.ds(base + PAD, 8), :] = f

    def halo_copies(k):
        return [
            pltpu.make_async_remote_copy(
                src_ref=sent.at[k, side],
                dst_ref=got.at[k, 1 - side],
                send_sem=halo_ss.at[k, side],
                recv_sem=halo_rs.at[k, 1 - side],
                device_id=(me, other),
                device_id_type=MESH,
            )
            for side, other in enumerate((up, down))
        ]

    def send_halo(k):
        @pl.loop(0, 2)
        def _(side):
            base = pl.multiple_of(side * (ROWS - 8), 8)
            from_edge = sublane + side * (7 - 2 * sublane)
            for c in range(PANELS):
                f0, f1 = (flux[p, c, pl.ds(base + PAD, 8), :] for p in range(2))
                h0, h1 = (state[p, 0, c, pl.ds(base + PAD, 8), :] for p in range(2))
                second = jnp.where(side == 0, pltpu.roll(h0, 2, 0), pltpu.roll(h0, 6, 0))
                fourth = jnp.where(side == 0, pltpu.roll(h1, 6, 0), pltpu.roll(h1, 2, 0))
                sent[k, side, c, :, :] = jnp.where(
                    from_edge < 4,
                    jnp.where(from_edge < 2, f0, second),
                    jnp.where(from_edge < 6, pltpu.roll(f1, 4, 0), fourth),
                )

        for copy in halo_copies(k):
            copy.start()

    def inner(k):
        last = 8 - k

        @pl.loop(0, last + 1)
        def _(i):
            low = 4 * k - 2 + 8 * i
            put_heights(low - 4 * (i // last), low, ROWS + 2 - 4 * k)

        @pl.loop(0, 8 - k)
        def _(i):
            put_velocities(4 * k + 8 * i)

    def outer(k):
        @pl.loop(0, 2 * k)
        def _(j):
            edge, i = j % 2, j // 2
            put_heights(edge * ROWS - 4 * k + 8 * i, edge * (ROWS + 2 - 4 * k) - (1 - edge) * PAD, 4 * k - 2 + edge * (ROWS + PAD))

        send_halo(k - 1)

        @pl.loop(0, 2 * k)
        def _(j):
            edge, i = j % 2, j // 2
            put_velocities(edge * ROWS - 4 * k + 8 * i)

    def whole(k):
        @pl.loop(0, 13 - k)
        def _(i):
            put_heights(4 * k - 18 + 8 * i, -PAD, 82 - 4 * k)

        send_halo(k - 1)

        @pl.loop(0, 12 - k)
        def _(i):
            put_velocities(4 * k - 16 + 8 * i)

    def other_part(k):
        for copy in halo_copies(k - 1):
            copy.wait_recv()
        third = k // 3
        for side in range(2):
            there = sp < 7 if side else sp > 0
            near = slice(24, 32) if side else slice(0, 8)
            for c in range(PANELS):
                message = jnp.where(there, got[k - 1, side, c, :, :], 0.0)
                for p in range(2):
                    part_flux[side, p, c, near, :] = pltpu.roll(message, 4, 0) if p else message
                    part[side, p, 0, c, near, :] = pltpu.roll(message, 2 if side == p else 6, 0)

        @pl.loop(0, 2 + 2 * third)
        def _(j):
            side, i = j % 2, j // 2
            at = pl.multiple_of(8 + 8 * (side + i - 2 * side * i), 8)
            here = pl.ds(at, 8)
            own = pl.ds(pl.multiple_of(PAD - 8 + at + side * (ROWS - 16), 8), 8)
            found = []
            for p in range(2):
                columns = columns_of([depth[c, own, :] * part[side, p, 1, c, here, :] for c in range(PANELS)])
                for c, along in enumerate(columns):
                    a = part_flux[side, p, c, pl.ds(at + 1, 8), :]
                    b = part_flux[side, p, c, pl.ds(at - 1, 8), :]
                    a2 = part_flux[side, p, c, pl.ds(at + 2, 8), :]
                    b2 = part_flux[side, p, c, pl.ds(at - 2, 8), :]
                    h = part[side, p, 0, c, here, :] - K * (along + (8.0 * (a - b) - (a2 - b2)))
                    found.append((p, c, keep[c, own, :] * h))
            for p, c, h in found:
                part[side, p, 0, c, here, :] = h

        @pl.loop(0, 2 + 2 * third)
        def _(j):
            side, i = j % 2, j // 2
            at = pl.multiple_of(8 + 8 * (side + i - 2 * side * i), 8)
            here = pl.ds(at, 8)
            own = pl.ds(pl.multiple_of(PAD - 8 + at + side * (ROWS - 16), 8), 8)
            found = []
            for p in range(2):
                for c, along in enumerate(columns_of([part[side, p, 0, c, here, :] for c in range(PANELS)])):
                    a = part[side, p, 0, c, pl.ds(at + 1, 8), :]
                    b = part[side, p, 0, c, pl.ds(at - 1, 8), :]
                    a2 = part[side, p, 0, c, pl.ds(at + 2, 8), :]
                    b2 = part[side, p, 0, c, pl.ds(at - 2, 8), :]
                    e, n = part[side, p, 1, c, here, :], part[side, p, 2, c, here, :]
                    e_new = e - K * along + (DT * F0) * n
                    n_new = n - K * (8.0 * (a - b) - (a2 - b2)) - (DT * F0) * e
                    found.append((p, c, e_new, n_new, depth[c, own, :] * n_new))
            for p, c, e, n, f in found:
                part[side, p, 1, c, here, :] = e
                part[side, p, 2, c, here, :] = n
                part_flux[side, p, c, here, :] = f

    def join():
        @pl.loop(0, 4)
        def _(j):
            side, i = j % 2, j // 2
            here = pl.ds(pl.multiple_of(8 + 8 * i, 8), 8)
            own = pl.ds(pl.multiple_of(PAD + 8 * i + side * (ROWS - 16), 8), 8)
            found = [
                (p, f, c, state[p, f, c, own, :] + part[side, p, f, c, here, :])
                for p in range(2) for f in range(3) for c in range(PANELS)
            ]
            for p, f, c, v in found:
                state[p, f, c, own, :] = v

    def own_collect(piece):
        return pltpu.make_async_copy(
            state.at[:, :, pl.ds(2 * quarter_of(me), 2), pl.ds(PAD + row_of(piece, me), 8), :],
            gathered[piece].at[pl.ds(2 * me, 2)],
            self_sem.at[piece],
        )

    def collect(piece, first=1, last=GROUP):
        @pl.loop(first, last)
        def _(i):
            d = peer_of(me, i)
            pltpu.make_async_remote_copy(
                src_ref=state.at[:, :, pl.ds(2 * quarter_of(d), 2), pl.ds(PAD + row_of(piece, d), 8), :],
                dst_ref=gathered[piece].at[pl.ds(2 * me, 2)],
                send_sem=ss1.at[piece],
                recv_sem=rs1.at[piece],
                device_id=(d, sp),
                device_id_type=MESH,
            ).start()

        if last == GROUP:
            own_collect(piece).start()

    def own_deliver(piece):
        return pltpu.make_async_copy(
            chosen.at[piece, pl.ds(2 * me, 2)],
            out.at[:, :, pl.ds(row_of(piece, me), 8), pl.ds(256 * quarter_of(me), 256)],
            self_sem.at[2 + piece],
        )

    def all_of(piece, sem):
        whole = gathered[piece].at[pl.ds(0, 30)]
        return pltpu.make_async_copy(whole, whole, sem.at[piece])

    def deliver(piece):
        all_of(piece, rs1).wait()
        own_collect(piece).wait()

        @pl.loop(0, 32)
        def _(j):
            source = copies[j]
            for f in range(3):
                for c in range(2):
                    chosen[piece, j, f, :, c * 128 : c * 128 + 128] = gathered[piece][source, f, c]

        @pl.loop(1, GROUP)
        def _(i):
            d = peer_of(me, i)
            pltpu.make_async_remote_copy(
                src_ref=chosen.at[piece, pl.ds(2 * d, 2)],
                dst_ref=out.at[:, :, pl.ds(row_of(piece, me), 8), pl.ds(256 * quarter_of(me), 256)],
                send_sem=ss2.at[piece],
                recv_sem=rs2.at[piece],
                device_id=(d, sp),
                device_id_type=MESH,
            ).start()

        own_deliver(piece).start()

    fixed = [
        pltpu.make_async_remote_copy(
            src_ref=ref.at[:, pl.ds(source, 8), :],
            dst_ref=ref.at[:, pl.ds(target, 8), :],
            send_sem=fixed_ss.at[n, side],
            recv_sem=fixed_rs.at[n, 1 - side],
            device_id=(me, other),
            device_id_type=MESH,
        )
        for n, ref in enumerate((depth, keep))
        for side, other, source, target in ((0, up, PAD, PAD + ROWS), (1, down, PAD + ROWS - 8, PAD - 8))
    ]

    def take_fixed():
        for copy in fixed:
            copy.wait_recv()
        for there, row in ((sp > 0, PAD - 8), (sp < 7, PAD + ROWS)):
            for ref in (depth, keep):
                for c in range(PANELS):
                    ref[c, row : row + 8, :] = jnp.where(there, ref[c, row : row + 8, :], 0.0)

    pl.semaphore_wait(barrier, GROUP + 1)
    for copy in fixed:
        copy.start()
    inner(1)
    inner(2)
    take_fixed()

    @pl.loop(1, 3)
    def _(k):
        outer(k)


    @pl.loop(3, STEPS + 1)
    def _(k):
        whole(k)

    collect(0)

    @pl.loop(1, STEPS + 1)
    def _(k):
        other_part(k)

    join()
    collect(1)
    deliver(0)
    deliver(1)
    for piece in range(2):
        all_of(piece, rs2).wait()
        own_deliver(piece).wait()
    for piece in range(2):
        all_of(piece, ss1).wait()
        all_of(piece, ss2).wait()
    for copy in fixed:
        copy.wait_send()

    @pl.loop(0, STEPS)
    def _(k):
        for copy in halo_copies(k):
            copy.wait_send()


def shards(particles, copies, depth_class, depth_table, observed, nudge_gain):
    f32 = jnp.float32
    sem = pltpu.SemaphoreType.DMA
    anywhere = pl.BlockSpec(memory_space=pl.ANY)
    return pl.pallas_call(
        kernel,
        out_shape=jax.ShapeDtypeStruct(particles.shape, f32),
        in_specs=[anywhere] * 6,
        out_specs=anywhere,
        scratch_shapes=[
            pltpu.SMEM((32,), jnp.int32),
            pltpu.SMEM((CLASSES,), f32),
            pltpu.VMEM((2, 3, ROWS, 1024), f32),
            pltpu.VMEM((ROWS, 1024), jnp.int32),
            pltpu.VMEM((ROWS, 1024), f32),
            pltpu.VMEM((ROWS, 1024), f32),
            pltpu.VMEM((PANELS, ROWS + 2 * PAD, 128), f32),
            pltpu.VMEM((PANELS, ROWS + 2 * PAD, 128), f32),
            pltpu.VMEM((PANELS, ROWS + 2 * PAD, 128), f32),
            pltpu.VMEM((2, 3, PANELS, ROWS + 2 * PAD, 128), f32),
            pltpu.VMEM((2, PANELS, ROWS + 2 * PAD, 128), f32),
            pltpu.VMEM((2, 2, 3, PANELS, 32, 128), f32),
            pltpu.VMEM((2, 2, PANELS, 32, 128), f32),
            pltpu.VMEM((32, 3, 2, 8, 128), f32),
            pltpu.VMEM((32, 3, 2, 8, 128), f32),
            pltpu.VMEM((2, 32, 3, 8, 256), f32),
            pltpu.VMEM((STEPS, 2, PANELS, 8, 128), f32),
            pltpu.VMEM((STEPS, 2, PANELS, 8, 128), f32),
            sem((6,)), sem((STEPS, 2)), sem((STEPS, 2)), sem((2, 2)), sem((2, 2)),
            sem((2,)), sem((2,)), sem((2,)), sem((2,)), sem((4,)),
        ],
        compiler_params=pltpu.CompilerParams(
            collective_id=0, has_side_effects=True, vmem_limit_bytes=60 * 2**20
        ),
    )(copies, depth_table, particles, depth_class, observed, nudge_gain)


def solution(mesh):
    placed = (
        P("dom", None, "space", None),
        P(),
        P("space", None),
        P(),
        P("space", None),
        P("space", None),
    )
    return jax.shard_map(
        shards, mesh=mesh, in_specs=placed, out_specs=P("dom", None, "space", None), check_vma=False
    )
```

profile of v0, /device:TPU:1, one launch (start us, length us, event | category | flops | bytes accessed | tf_op | source)
XLA Modules:
  0.0 60.2 jit_solution(11606965919147404996)
XLA Ops:
  0.0 57.5 %shard_map.64 = f32[2,3,64,1024]{3,2,1,0:T(8,128)} custom-call(s32[32]{0:T(128)} %copies_in.1, f32[8]{0:T(128)} %table_in.1, f32[2,3,64,1024]{3,2,1,0:T(8,128)} %particles.1, s32[64,1024]{1,0:T(8,128)} %classes.1, f32[64,1024]{1,0:T(8,128)} %observed.1, f32[64,1024]{1,0:T(8,128)} %gain.1), custom_call_target="tpu_custom_call" | custom-call | tf_op jit(solution)/shard_map/pallas_call | solution.py:448
  57.5 2.7 %copy.8 = f32[2,3,64,1024]{3,2,1,0:T(8,128)} copy(f32[2,3,64,1024]{3,2,1,0:T(8,128)} %shard_map.64) | data formatting | bytes 3145728
where the time goes:
time: 60.4 us; the launch traced here: 60.2 us
  Pallas kernels  57.5 us (95%)
  local copies, waits for them, and re-layouts  2.73 us (5%)
    pallas_call x1, Pallas kernels, shards(): pl.pallas_call(kernel, out_shape=jax.ShapeDtypeStruct(particles.shape, f3...  57.5 us
    unnamed x1, local copies, waits for them, and re-layouts  2.73 us

commit v1 on v0

--- a/solution.py
+++ b/solution.py
@@ -38,7 +38,7 @@
 
 def kernel(
     copies_in, table_in, particles, classes, observed, gain, out,
-    copies, table, stage, cls, obs, gn, depth, keep, drive, state, flux, part, part_flux, gathered0, gathered1, chosen, sent, got,
+    copies, table, stage, cls, obs, gn, depth, keep, drive, state, flux, part, part_flux, band, gathered0, gathered1, chosen, sent, got,
     load_sem, halo_ss, halo_rs, fixed_ss, fixed_rs, ss1, rs1, ss2, rs2, self_sem,
 ):
     me, sp = lax.axis_index("dom"), lax.axis_index("space")
@@ -67,6 +67,13 @@
 
     lane = lax.broadcasted_iota(jnp.int32, (8, 128), 1)
     sublane = lax.broadcasted_iota(jnp.int32, (8, 128), 0)
+
+    row = lax.broadcasted_iota(jnp.int32, (512, 128), 0) % 256
+    column = lax.broadcasted_iota(jnp.int32, (512, 128), 1)
+    ahead = row - jnp.where(column < 64, column + 128, column)
+    weights = jnp.where(ahead == 1, 8.0, 0.0) - jnp.where(ahead == -1, 8.0, 0.0)
+    weights = weights - jnp.where(ahead == 2, 1.0, 0.0) + jnp.where(ahead == -2, 1.0, 0.0)
+    band[...] = weights.astype(jnp.bfloat16)
 
     loads[0].wait()
     loads[4].wait()
@@ -143,47 +150,83 @@
     def columns_of(panels):
         return [8.0 * (a - b) - (a2 - b2) for a, b, a2, b2 in shifts(panels)]
 
-    def heights_of(base, low, high):
-        inside = (base + sublane >= low) & (base + sublane < high)
-        here = pl.ds(base + PAD, 8)
+    def split_columns(panels):
+        parts = []
+        for c in range(PANELS):
+            v = jnp.concatenate([panels[0][c], panels[1][c]], axis=0)
+            high = v.astype(jnp.bfloat16)
+            parts.append((high, (v - high.astype(jnp.float32)).astype(jnp.bfloat16)))
+        rows = []
+        for c in range(PANELS):
+            here, ahead = parts[c], parts[(c + 1) % PANELS]
+            rows.append(jnp.concatenate([here[0], ahead[0], here[1], ahead[1]], axis=1))
+        product = jnp.dot(jnp.concatenate(rows, axis=0), band[...], preferred_element_type=jnp.float32)
+        pieces = [product[16 * c : 16 * c + 16] for c in range(PANELS)]
+        wide = lax.broadcasted_iota(jnp.int32, (16, 128), 1)
+        found = [jnp.where(wide < 64, pieces[c - 1], pieces[c]) for c in range(PANELS)]
+        return [v[:8] for v in found], [v[8:] for v in found]
+
+    def all_columns(panels):
+        if len(panels[0]) == 1:
+            return [[columns_of(panels[p][0])] for p in range(2)]
+        return [[columns_of(v) for v in panels[0]], split_columns(panels[1])]
+
+    def put_heights(*windows):
+        heres = [pl.ds(base + PAD, 8) for base, _, _ in windows]
+        columns = all_columns(
+            [[[depth[c, here, :] * state[p, 1, c, here, :] for c in range(PANELS)] for here in heres] for p in range(2)]
+        )
         found = []
         for p in range(2):
-            columns = columns_of([depth[c, here, :] * state[p, 1, c, here, :] for c in range(PANELS)])
-            for c, along in enumerate(columns):
-                a = flux[p, c, pl.ds(base + PAD + 1, 8), :]
-                b = flux[p, c, pl.ds(base + PAD - 1, 8), :]
-                a2 = flux[p, c, pl.ds(base + PAD + 2, 8), :]
-                b2 = flux[p, c, pl.ds(base + PAD - 2, 8), :]
-                old = state[p, 0, c, here, :]
-                h = old - K * (along + (8.0 * (a - b) - (a2 - b2)))
-                h = keep[c, here, :] * h + drive[c, here, :]
-                found.append((p, c, jnp.where(inside, h, old)))
-        return found
-
-    def put_heights(base, low, high):
-        for p, c, h in heights_of(base, low, high):
-            state[p, 0, c, pl.ds(base + PAD, 8), :] = h
-
-    def velocities_of(base):
-        here = pl.ds(base + PAD, 8)
+            for w, (base, low, high) in enumerate(windows):
+                inside = (base + sublane >= low) & (base + sublane < high)
+                here = heres[w]
+                for c, along in enumerate(columns[p][w]):
+                    a = flux[p, c, pl.ds(base + PAD + 1, 8), :]
+                    b = flux[p, c, pl.ds(base + PAD - 1, 8), :]
+                    a2 = flux[p, c, pl.ds(base + PAD + 2, 8), :]
+                    b2 = flux[p, c, pl.ds(base + PAD - 2, 8), :]
+                    old = state[p, 0, c, here, :]
+                    h = old - K * (along + (8.0 * (a - b) - (a2 - b2)))
+                    h = keep[c, here, :] * h + drive[c, here, :]
+                    found.append((p, c, here, jnp.where(inside, h, old)))
+        for p, c, here, h in found:
+            state[p, 0, c, here, :] = h
+
+    def put_velocities(*bases):
+        heres = [pl.ds(base + PAD, 8) for base in bases]
+        columns = all_columns([[[state[p, 0, c, here, :] for c in range(PANELS)] for here in heres] for p in range(2)])
         found = []
         for p in range(2):
-            for c, along in enumerate(columns_of([state[p, 0, c, here, :] for c in range(PANELS)])):
-                a = state[p, 0, c, pl.ds(base + PAD + 1, 8), :]
-                b = state[p, 0, c, pl.ds(base + PAD - 1, 8), :]
-                a2 = state[p, 0, c, pl.ds(base + PAD + 2, 8), :]
-                b2 = state[p, 0, c, pl.ds(base + PAD - 2, 8), :]
-                e, n = state[p, 1, c, here, :], state[p, 2, c, here, :]
-                e_new = e - K * along + (DT * F0) * n
-                n_new = n - K * (8.0 * (a - b) - (a2 - b2)) - (DT * F0) * e
-                found.append((p, c, e_new, n_new, depth[c, here, :] * n_new))
-        return found
-
-    def put_velocities(base):
-        for p, c, e, n, f in velocities_of(base):
-            state[p, 1, c, pl.ds(base + PAD, 8), :] = e
-            state[p, 2, c, pl.ds(base + PAD, 8), :] = n
-            flux[p, c, pl.ds(base + PAD, 8), :] = f
+            for w, base in enumerate(bases):
+                here = heres[w]
+                for c, along in enumerate(columns[p][w]):
+                    a = state[p, 0, c, pl.ds(base + PAD + 1, 8), :]
+                    b = state[p, 0, c, pl.ds(base + PAD - 1, 8), :]
+                    a2 = state[p, 0, c, pl.ds(base + PAD + 2, 8), :]
+                    b2 = state[p, 0, c, pl.ds(base + PAD - 2, 8), :]
+                    e, n = state[p, 1, c, here, :], state[p, 2, c, here, :]
+                    e_new = e - K * along + (DT * F0) * n
+                    n_new = n - K * (8.0 * (a - b) - (a2 - b2)) - (DT * F0) * e
+                    found.append((p, c, here, e_new, n_new, depth[c, here, :] * n_new))
+        for p, c, here, e, n, f in found:
+            state[p, 1, c, here, :] = e
+            state[p, 2, c, here, :] = n
+            flux[p, c, here, :] = f
+
+    def in_pairs(count, put, window):
+        @pl.loop(0, count // 2)
+        def _(i):
+            put(window(i), window(i + count // 2))
+
+        if count % 2:
+            put(window(count - 1))
+
+    def height_windows(count, window):
+        in_pairs(count, put_heights, window)
+
+    def velocity_windows(count, first):
+        in_pairs(count, put_velocities, lambda i: first + 8 * i)
 
     def halo_copies(k):
         return [
@@ -220,38 +263,30 @@
     def inner(k):
         last = 8 - k
 
-        @pl.loop(0, last + 1)
-        def _(i):
+        def window(i):
             low = 4 * k - 2 + 8 * i
-            put_heights(low - 4 * (i // last), low, ROWS + 2 - 4 * k)
-
-        @pl.loop(0, 8 - k)
-        def _(i):
-            put_velocities(4 * k + 8 * i)
+            return low - 4 * (i // last), low, ROWS + 2 - 4 * k
+
+        height_windows(last + 1, window)
+        velocity_windows(8 - k, 4 * k)
 
     def outer(k):
-        @pl.loop(0, 2 * k)
-        def _(j):
-            edge, i = j % 2, j // 2
-            put_heights(edge * ROWS - 4 * k + 8 * i, edge * (ROWS + 2 - 4 * k) - (1 - edge) * PAD, 4 * k - 2 + edge * (ROWS + PAD))
+        @pl.loop(0, k)
+        def _(i):
+            put_heights(
+                (8 * i - 4 * k, -PAD, 4 * k - 2), (ROWS - 4 * k + 8 * i, ROWS + 2 - 4 * k, ROWS + PAD)
+            )
 
         send_halo(k - 1)
 
-        @pl.loop(0, 2 * k)
-        def _(j):
-            edge, i = j % 2, j // 2
-            put_velocities(edge * ROWS - 4 * k + 8 * i)
+        @pl.loop(0, k)
+        def _(i):
+            put_velocities(8 * i - 4 * k, ROWS - 4 * k + 8 * i)
 
     def whole(k):
-        @pl.loop(0, 13 - k)
-        def _(i):
-            put_heights(4 * k - 18 + 8 * i, -PAD, 82 - 4 * k)
-
+        height_windows(13 - k, lambda i: (4 * k - 18 + 8 * i, -PAD, 82 - 4 * k))
         send_halo(k - 1)
-
-        @pl.loop(0, 12 - k)
-        def _(i):
-            put_velocities(4 * k - 16 + 8 * i)
+        velocity_windows(12 - k, 4 * k - 16)
 
     def other_part(k):
         for copy in halo_copies(k - 1):
@@ -266,43 +301,51 @@
                     part_flux[side, p, c, near, :] = pltpu.roll(message, 4, 0) if p else message
                     part[side, p, 0, c, near, :] = pltpu.roll(message, 2 if side == p else 6, 0)
 
-        @pl.loop(0, 2 + 2 * third)
-        def _(j):
-            side, i = j % 2, j // 2
-            at = pl.multiple_of(8 + 8 * (side + i - 2 * side * i), 8)
-            here = pl.ds(at, 8)
-            own = pl.ds(pl.multiple_of(PAD - 8 + at + side * (ROWS - 16), 8), 8)
+        @pl.loop(0, 1 + third)
+        def _(i):
+            ats = (pl.multiple_of(8 + 8 * i, 8), pl.multiple_of(16 - 8 * i, 8))
+            heres = [pl.ds(at, 8) for at in ats]
+            owns = [pl.ds(pl.multiple_of(PAD - 8 + at + side * (ROWS - 16), 8), 8) for side, at in enumerate(ats)]
+            columns = all_columns([
+                [[depth[c, owns[side], :] * part[side, p, 1, c, heres[side], :] for c in range(PANELS)] for side in range(2)]
+                for p in range(2)
+            ])
             found = []
             for p in range(2):
-                columns = columns_of([depth[c, own, :] * part[side, p, 1, c, here, :] for c in range(PANELS)])
-                for c, along in enumerate(columns):
-                    a = part_flux[side, p, c, pl.ds(at + 1, 8), :]
-                    b = part_flux[side, p, c, pl.ds(at - 1, 8), :]
-                    a2 = part_flux[side, p, c, pl.ds(at + 2, 8), :]
-                    b2 = part_flux[side, p, c, pl.ds(at - 2, 8), :]
-                    h = part[side, p, 0, c, here, :] - K * (along + (8.0 * (a - b) - (a2 - b2)))
-                    found.append((p, c, keep[c, own, :] * h))
-            for p, c, h in found:
+                for side, at in enumerate(ats):
+                    here, own = heres[side], owns[side]
+                    for c, along in enumerate(columns[p][side]):
+                        a = part_flux[side, p, c, pl.ds(at + 1, 8), :]
+                        b = part_flux[side, p, c, pl.ds(at - 1, 8), :]
+                        a2 = part_flux[side, p, c, pl.ds(at + 2, 8), :]
+                        b2 = part_flux[side, p, c, pl.ds(at - 2, 8), :]
+                        h = part[side, p, 0, c, here, :] - K * (along + (8.0 * (a - b) - (a2 - b2)))
+                        found.append((side, p, c, here, keep[c, own, :] * h))
+            for side, p, c, here, h in found:
                 part[side, p, 0, c, here, :] = h
 
-        @pl.loop(0, 2 + 2 * third)
-        def _(j):
-            side, i = j % 2, j // 2
-            at = pl.multiple_of(8 + 8 * (side + i - 2 * side * i), 8)
-            here = pl.ds(at, 8)
-            own = pl.ds(pl.multiple_of(PAD - 8 + at + side * (ROWS - 16), 8), 8)
+        @pl.loop(0, 1 + third)
+        def _(i):
+            ats = (pl.multiple_of(8 + 8 * i, 8), pl.multiple_of(16 - 8 * i, 8))
+            heres = [pl.ds(at, 8) for at in ats]
+            owns = [pl.ds(pl.multiple_of(PAD - 8 + at + side * (ROWS - 16), 8), 8) for side, at in enumerate(ats)]
+            columns = all_columns([
+                [[part[side, p, 0, c, heres[side], :] for c in range(PANELS)] for side in range(2)] for p in range(2)
+            ])
             found = []
             for p in range(2):
-                for c, along in enumerate(columns_of([part[side, p, 0, c, here, :] for c in range(PANELS)])):
-                    a = part[side, p, 0, c, pl.ds(at + 1, 8), :]
-                    b = part[side, p, 0, c, pl.ds(at - 1, 8), :]
-                    a2 = part[side, p, 0, c, pl.ds(at + 2, 8), :]
-                    b2 = part[side, p, 0, c, pl.ds(at - 2, 8), :]
-                    e, n = part[side, p, 1, c, here, :], part[side, p, 2, c, here, :]
-                    e_new = e - K * along + (DT * F0) * n
-                    n_new = n - K * (8.0 * (a - b) - (a2 - b2)) - (DT * F0) * e
-                    found.append((p, c, e_new, n_new, depth[c, own, :] * n_new))
-            for p, c, e, n, f in found:
+                for side, at in enumerate(ats):
+                    here, own = heres[side], owns[side]
+                    for c, along in enumerate(columns[p][side]):
+                        a = part[side, p, 0, c, pl.ds(at + 1, 8), :]
+                        b = part[side, p, 0, c, pl.ds(at - 1, 8), :]
+                        a2 = part[side, p, 0, c, pl.ds(at + 2, 8), :]
+                        b2 = part[side, p, 0, c, pl.ds(at - 2, 8), :]
+                        e, n = part[side, p, 1, c, here, :], part[side, p, 2, c, here, :]
+                        e_new = e - K * along + (DT * F0) * n
+                        n_new = n - K * (8.0 * (a - b) - (a2 - b2)) - (DT * F0) * e
+                        found.append((side, p, c, here, e_new, n_new, depth[c, own, :] * n_new))
+            for side, p, c, here, e, n, f in found:
                 part[side, p, 1, c, here, :] = e
                 part[side, p, 2, c, here, :] = n
                 part_flux[side, p, c, here, :] = f
@@ -406,16 +449,10 @@
     inner(1)
     inner(2)
     take_fixed()
-
-    @pl.loop(1, 3)
-    def _(k):
-        outer(k)
-
-
-    @pl.loop(3, STEPS + 1)
-    def _(k):
-        whole(k)
-
+    outer(1)
+    outer(2)
+    whole(3)
+    whole(4)
     collect(0)
 
     @pl.loop(1, STEPS + 1)
@@ -464,6 +501,7 @@
             pltpu.VMEM((2, PANELS, ROWS + 2 * PAD, 128), f32),
             pltpu.VMEM((2, 2, 3, PANELS, 32, 128), f32),
             pltpu.VMEM((2, 2, PANELS, 32, 128), f32),
+            pltpu.VMEM((512, 128), jnp.bfloat16),
             pltpu.VMEM((32, 3, 2, 8, 128), f32),
             pltpu.VMEM((32, 3, 2, 8, 128), f32),
             pltpu.VMEM((2, 32, 3, 8, 256), f32),

time: 60.4 us -> 58.3 us (0.965)
  Pallas kernels: 57.5 us -> 55.4 us
    pallas_call x1, Pallas kernels: 57.5 us -> 55.4 us  [shards(): pl.pallas_call(kernel, out_shape=jax.ShapeDtypeStruct(particles.shape, f3...]
where the time goes in v1:
time: 58.3 us; the launch traced here: 58.2 us
  Pallas kernels  55.4 us (95%)
  local copies, waits for them, and re-layouts  2.73 us (5%)
    pallas_call x1, Pallas kernels, shards(): pl.pallas_call(kernel, out_shape=jax.ShapeDtypeStruct(particles.shape, f3...  55.4 us
    unnamed x1, local copies, waits for them, and re-layouts  2.73 us

profile of v1, /device:TPU:1, one launch (start us, length us, event | category | flops | bytes accessed | tf_op | source)
XLA Modules:
  0.0 58.2 jit_solution(12132370784969527133)
XLA Ops:
  0.0 55.4 %shard_map.64 = f32[2,3,64,1024]{3,2,1,0:T(8,128)} custom-call(s32[32]{0:T(128)} %copies_in.1, f32[8]{0:T(128)} %table_in.1, f32[2,3,64,1024]{3,2,1,0:T(8,128)} %particles.1, s32[64,1024]{1,0:T(8,128)} %classes.1, f32[64,1024]{1,0:T(8,128)} %observed.1, f32[64,1024]{1,0:T(8,128)} %gain.1), custom_call_target="tpu_custom_call" | custom-call | tf_op jit(solution)/shard_map/pallas_call | solution.py:485
  55.4 2.7 %copy.8 = f32[2,3,64,1024]{3,2,1,0:T(8,128)} copy(f32[2,3,64,1024]{3,2,1,0:T(8,128)} %shard_map.64) | data formatting | bytes 3145728

commit v2 on v1

--- a/solution.py
+++ b/solution.py
@@ -401,16 +401,17 @@
         all_of(piece, rs1).wait()
         own_collect(piece).wait()
 
-        @pl.loop(0, 32)
-        def _(j):
-            source = copies[j]
-            for f in range(3):
-                for c in range(2):
-                    chosen[piece, j, f, :, c * 128 : c * 128 + 128] = gathered[piece][source, f, c]
+        def pick(d):
+            sources = [copies[2 * d + slot] for slot in range(2)]
+            picked = [gathered[piece][source, f, c] for source in sources for f in range(3) for c in range(2)]
+            for n, v in enumerate(picked):
+                f, c = n // 2 % 3, n % 2
+                chosen[piece, 2 * d + n // 6, f, :, c * 128 : c * 128 + 128] = v
 
         @pl.loop(1, GROUP)
         def _(i):
             d = peer_of(me, i)
+            pick(d)
             pltpu.make_async_remote_copy(
                 src_ref=chosen.at[piece, pl.ds(2 * d, 2)],
                 dst_ref=out.at[:, :, pl.ds(row_of(piece, me), 8), pl.ds(256 * quarter_of(me), 256)],
@@ -420,6 +421,7 @@
                 device_id_type=MESH,
             ).start()
 
+        pick(me)
         own_deliver(piece).start()
 
     fixed = [

time: 58.3 us -> 58.3 us (level)
  no operation moved by 1% of the time
where the time goes in v2:
time: 58.3 us; the launch traced here: 58.2 us
  Pallas kernels  55.4 us (95%)
  local copies, waits for them, and re-layouts  2.73 us (5%)
    pallas_call x1, Pallas kernels, shards(): pl.pallas_call(kernel, out_shape=jax.ShapeDtypeStruct(particles.shape, f3...  55.4 us
    unnamed x1, local copies, waits for them, and re-layouts  2.73 us

profile of v2, /device:TPU:1, one launch (start us, length us, event | category | flops | bytes accessed | tf_op | source)
XLA Modules:
  0.0 58.2 jit_solution(8659137734869549324)
XLA Ops:
  0.0 55.4 %shard_map.64 = f32[2,3,64,1024]{3,2,1,0:T(8,128)} custom-call(s32[32]{0:T(128)} %copies_in.1, f32[8]{0:T(128)} %table_in.1, f32[2,3,64,1024]{3,2,1,0:T(8,128)} %particles.1, s32[64,1024]{1,0:T(8,128)} %classes.1, f32[64,1024]{1,0:T(8,128)} %observed.1, f32[64,1024]{1,0:T(8,128)} %gain.1), custom_call_target="tpu_custom_call" | custom-call | tf_op jit(solution)/shard_map/pallas_call | solution.py:487
  55.4 2.7 %copy.8 = f32[2,3,64,1024]{3,2,1,0:T(8,128)} copy(f32[2,3,64,1024]{3,2,1,0:T(8,128)} %shard_map.64) | data formatting | bytes 3145728
